TPU v7x, 128 devices: a whole 4x4x4 slice. The times are simulated.
128 devices in a mesh: dp: 16 (over x, z_hi, core), tensor: 8 (over y, z_lo).
Axes of the slice: x: 4, y: 4, z: 4 (z_hi: 2, z_lo: 2; z = z_hi * 2 + z_lo), core: 2. Of those that a mesh axis runs over, the one named last changes fastest.
Arguments:
- inputs: bfloat16 [1024, 12288], P('tensor', 'dp'), may hold values from -11 to 14, as said below
- norm_gain: float32 [12288], P('dp'), may hold values from 0.5 to 1.5
- norm_bias: float32 [12288], P('dp'), may hold values from -3 to 3
- w_up: bfloat16 [12288, 24576], P('dp', 'tensor'), may hold values from -0.0546875 to 0.0546875
- b_up: float32 [24576], P('tensor'), may hold values from -3 to 3
- w_down: bfloat16 [24576, 12288], P('tensor', 'dp'), may hold values from -0.0390625 to 0.0390625
- b_down: float32 [12288], P('dp'), may hold values from -3 to 3
- d_branch: bfloat16 [1024, 12288], P('tensor', 'dp'), may hold values from -6 to 6
Outputs:
- branch: bfloat16 [1024, 12288], P('tensor', 'dp')
- grad_inputs: bfloat16 [1024, 12288], P('tensor', 'dp')
- grad_w_up: bfloat16 [12288, 24576], P('dp', 'tensor')
- grad_b_up: float32 [24576], P('tensor')
- grad_w_down: bfloat16 [24576, 12288], P('tensor', 'dp')
- grad_b_down: float32 [12288], P('dp')
- grad_gain: float32 [12288], P('dp')
- grad_bias: float32 [12288], P('dp')
Inputs may be any that keep to these rules, and one draw needn't show every extreme that they name: inputs are finite values of the residual stream.
All inputs are finite; a program needn't handle non-finite values.
Results may differ from a plain program's by a relative error of at most 0.025.
Values may be sent and summed in bfloat16 or wider, within the bound.
A program may use at most 128 MiB of HBM per device.

v0:
```python
import jax
import jax.numpy as jnp
from jax import lax
from jax.sharding import PartitionSpec as P

D = 12288


def gelu_tanh(value):
    return jax.nn.gelu(value, approximate=True)


def on_device(inputs, norm_gain, norm_bias, w_up, b_up, w_down, b_down, d_branch):
    widened = inputs.astype(jnp.float32)
    centre = lax.psum(jnp.sum(widened, axis=1, keepdims=True), "dp") / D
    centred = widened - centre
    spread = lax.psum(jnp.sum(centred * centred, axis=1, keepdims=True), "dp") / D
    inverse = lax.rsqrt(spread + 1e-05)
    standard = centred * inverse
    normed = (standard * norm_gain + norm_bias).astype(jnp.bfloat16)
    gathered = lax.all_gather(normed, "tensor", axis=0, tiled=True)
    partial_up = jnp.dot(gathered, w_up, preferred_element_type=jnp.float32)
    grad_rows = lax.all_gather(d_branch, "tensor", axis=0, tiled=True)
    hidden_pre = lax.psum(partial_up.astype(jnp.bfloat16), "dp").astype(jnp.float32) + b_up
    act = gelu_tanh(hidden_pre).astype(jnp.bfloat16)
    rows_part = act
    branch = (
        lax.psum_scatter(
            jnp.dot(rows_part, w_down, preferred_element_type=jnp.float32).astype(jnp.bfloat16),
            "tensor",
            scatter_dimension=0,
            tiled=True,
        ).astype(jnp.float32)
        + b_down
    ).astype(jnp.bfloat16)
    partial_back = lax.dot_general(
        grad_rows, w_down, (((1,), (1,)), ((), ())), preferred_element_type=jnp.float32
    )
    _, pullback = jax.vjp(gelu_tanh, hidden_pre)
    grad_act = lax.psum(partial_back.astype(jnp.bfloat16), "dp").astype(jnp.float32)
    grad_hidden = pullback(grad_act)[0].astype(jnp.bfloat16)
    grad_w_down = lax.dot_general(
        act, grad_rows, (((0,), (0,)), ((), ())), preferred_element_type=jnp.float32
    ).astype(jnp.bfloat16)
    grad_b_down = jnp.sum(grad_rows.astype(jnp.float32), axis=0)
    grad_w_up = lax.dot_general(
        gathered, grad_hidden, (((0,), (0,)), ((), ())), preferred_element_type=jnp.float32
    ).astype(jnp.bfloat16)
    grad_b_up = jnp.sum(grad_hidden.astype(jnp.float32), axis=0)
    rows_part = grad_hidden
    grad_normed = lax.psum_scatter(
        lax.dot_general(
            rows_part, w_up, (((1,), (1,)), ((), ())), preferred_element_type=jnp.float32
        ).astype(jnp.bfloat16),
        "tensor",
        scatter_dimension=0,
        tiled=True,
    ).astype(jnp.float32)
    grad_gain, grad_bias = lax.psum(
        (jnp.sum(grad_normed * standard, axis=0), jnp.sum(grad_normed, axis=0)), "tensor"
    )
    scaled = grad_normed * norm_gain
    back = lax.psum(
        (jnp.sum(scaled, axis=1, keepdims=True), jnp.sum(scaled * standard, axis=1, keepdims=True)),
        "dp",
    )
    grad_inputs = inverse * (scaled - back[0] / D - standard * (back[1] / D))
    return (
        branch,
        grad_inputs.astype(jnp.bfloat16),
        grad_w_up,
        grad_b_up,
        grad_w_down,
        grad_b_down,
        grad_gain,
        grad_bias,
    )


def solution(mesh):
    placed = (
        P("tensor", "dp"),
        P("dp"),
        P("dp"),
        P("dp", "tensor"),
        P("tensor"),
        P("tensor", "dp"),
        P("dp"),
        P("tensor", "dp"),
    )
    return jax.shard_map(
        on_device,
        mesh=mesh,
        in_specs=placed,
        out_specs=(
            P("tensor", "dp"),
            P("tensor", "dp"),
            P("dp", "tensor"),
            P("tensor"),
            P("tensor", "dp"),
            P("dp"),
            P("dp"),
            P("dp"),
        ),
        check_vma=False,
    )
```

profile of v0, /device:TPU:1, one launch (start us, length us, event | category | flops | bytes accessed | tf_op | source)
XLA Modules:
  0.0 591.3 jit_solution(4195250135129390390)
XLA Ops:
  7.2 0.0 all-gather.3.cloned.1.call-start
  7.2 1.0 convert_reduce_fusion.3
  8.3 34.8 %psum.56 = f32[128,1]{0,1:T(1,128)S(1)} all-reduce(f32[128,1]{0,1:T(1,128)S(1)} %bitcast.26), channel_id=1, replica_groups=mesh['dp'=16,'tensor'=8] {'dp'}, use_global_device_ids=true, to_apply=%region_1.0 | all-reduce | flops 128 | bytes 1024 | tf_op jit(solution)/shard_map/psum | solution.py:15
  43.1 1.1 fusion.24
  44.2 37.8 %psum.57 = f32[128,1]{0,1:T(1,128)S(1)} all-reduce(f32[128,1]{0,1:T(1,128)S(1)} %bitcast.27), channel_id=1, replica_groups=mesh['dp'=16,'tensor'=8] {'dp'}, use_global_device_ids=true, to_apply=%region_3.0 | all-reduce | flops 128 | bytes 1024 | tf_op jit(solution)/shard_map/psum | solution.py:17
  82.1 1.8 fusion.20
  83.9 0.0 all-gather.3.cloned.1.call-update
  83.9 0.0 all-gather.5.cloned.1.call-start
  83.9 0.7 all-gather.5.cloned.1.call-update
  84.6 0.0 all-reduce.5.cloned.1.call-start
  84.7 38.4 %all-gather.3.cloned.1.call-done = bf16[1024,768]{1,0:T(8,128)(2,1)} async-done(((bf16[128,768]{1,0:T(8,128)(2,1)}), bf16[1024,768]{1,0:T(8,128)(2,1)}) %all-gather.3.cloned.1.call-update) | async-done | bytes 1572880 | tf_op jit(solution)/shard_map/all_gather | solution.py:21
  123.1 9.0 %convolution_convert_fusion.1 = bf16[1024,3072]{1,0:T(8,128)(2,1)} fusion(bf16[1024,768]{1,0:T(8,128)(2,1)} %all-gather.3.cloned.1.call-done, bf16[768,3072]{1,0:T(8,128)(2,1)} %param.11), kind=kOutput, calls=%fused_computation.20 | convolution fusion | flops 4834983936 | bytes 12582912 | tf_op jit(solution)/shard_map/dot_general | solution.py:22
  132.2 36.2 %all-gather.5.cloned.1.call-done = bf16[1024,768]{1,0:T(8,128)(2,1)} async-done(((bf16[128,768]{1,0:T(8,128)(2,1)}), bf16[1024,768]{1,0:T(8,128)(2,1)}) %all-gather.5.cloned.1.call-update) | async-done | bytes 1572880 | tf_op jit(solution)/shard_map/all_gather | solution.py:23
  168.4 9.1 %convolution_convert_fusion = bf16[1024,3072]{1,0:T(8,128)(2,1)} fusion(bf16[1024,768]{1,0:T(8,128)(2,1)} %all-gather.5.cloned.1.call-done, bf16[3072,768]{1,0:T(8,128)(2,1)} %param.13), kind=kOutput, calls=%fused_computation.19 | convolution fusion | flops 4834983936 | bytes 12582912 | tf_op jit(solution)/shard_map/dot_general | solution.py:36
  177.5 0.0 copy-start.5
  177.5 0.0 all-reduce.5.cloned.1.call-update
  177.6 0.0 reduce-scatter.5.cloned.1.call-start
  177.6 284.7 %all-reduce.5.cloned.1.call-done = (bf16[1024,3072]{1,0:T(8,128)(2,1)}, bf16[1024,3072]{1,0:T(8,128)(2,1)}) async-done(((bf16[1024,3072]{1,0:T(8,128)(2,1)}, bf16[1024,3072]{1,0:T(8,128)(2,1)}), (bf16[1024,3072]{1,0:T(8,128)(2,1)}, bf16[1024,3072]{1,0:T(8,128)(2,1)})) %all-reduce.5.cloned.1.call-update) | async-done | bytes 12582928 | tf_op jit(solution)/shard_map/psum | solution.py:24
  462.3 0.0 copy-done.5
  462.3 12.8 %convert_reduce_fusion = (f32[3072]{0:T(1024)}, bf16[1024,3072]{1,0:T(8,128)(2,1)S(1)}) fusion(f32[3072]{0:T(1024)S(1)} %copy-done.5, bf16[1024,3072]{1,0:T(8,128)(2,1)} %get-tuple-element.16, bf16[1024,3072]{1,0:T(8,128)(2,1)} %get-tuple-element.17), kind=kLoop, calls=%fused_computation.14 | loop fusion | flops 78640128 | bytes 18898944 | tf_op jit(solution)/shard_map/reduce_sum | solution.py:49
  475.1 0.0 copy-start
  475.1 2.7 copy-done
  477.7 0.0 copy-start.2
  477.7 8.7 %convolution_convert_fusion.4 = bf16[1024,768]{1,0:T(8,128)(2,1)} fusion(bf16[1024,3072]{1,0:T(8,128)(2,1)S(1)} %get-tuple-element.19, bf16[768,3072]{1,0:T(8,128)(2,1)} %param.11), kind=kOutput, calls=%fused_computation.24 | convolution fusion | flops 4832624640 | bytes 12582912 | tf_op jit(solution)/shard_map/dot_general | solution.py:52
  486.4 0.0 reduce-scatter.5.cloned.1.call-update
  486.4 0.2 reduce-scatter.3.cloned.1.call-start
  486.6 0.0 copy-done.2
  486.7 0.9 convert_reduce_fusion.1
  487.5 12.4 %convolution_convert_fusion.5 = bf16[1024,768]{1,0:T(8,128)(2,1)} fusion(bf16[3072,768]{1,0:T(8,128)(2,1)} %param.13, bf16[1024,3072]{1,0:T(8,128)(2,1)} %get-tuple-element.16, f32[3072]{0:T(1024)S(1)} %copy-done.5), kind=kOutput, calls=%fused_computation.25 | convolution fusion | flops 4867227648 | bytes 12595200 | tf_op jit(solution)/shard_map/dot_general | solution.py:29
  500.0 0.0 slice-start
  500.0 0.0 reduce-scatter.3.cloned.1.call-update
  500.0 0.0 slice-start.1
  500.0 0.0 copy-start.3
  500.0 9.3 %convolution_convert_fusion.3 = bf16[768,3072]{1,0:T(8,128)(2,1)} fusion(bf16[1024,768]{1,0:T(8,128)(2,1)} %all-gather.3.cloned.1.call-done, bf16[1024,3072]{1,0:T(8,128)(2,1)} %copy-done), kind=kOutput, calls=%fused_computation.22 | convolution fusion | flops 4834197504 | bytes 12582912 | tf_op jit(solution)/shard_map/dot_general | solution.py:46
  509.3 0.0 slice-done
  509.3 0.0 slice-done.1
  509.3 0.0 copy-done.3
  509.3 0.0 copy-start.1
  509.3 0.0 copy-start.4
  509.3 0.0 copy-start.6
  509.3 9.9 %convolution_convert_fusion.2 = bf16[3072,768]{1,0:T(8,128)(2,1)} fusion(bf16[1024,768]{1,0:T(8,128)(2,1)S(1)} %copy-done.3, bf16[1024,3072]{1,0:T(8,128)(2,1)S(1)} %bitcast.23, f32[3072]{0:T(1024)S(1)} %copy-done.5), kind=kOutput, calls=%fused_computation.21 | convolution fusion | flops 4868800512 | bytes 12595200 | tf_op jit(solution)/shard_map/dot_general | solution.py:42
  519.2 8.1 %reduce-scatter.5.cloned.1.call-done = bf16[128,768]{1,0:T(8,128)(2,1)} async-done(((bf16[1024,768]{1,0:T(8,128)(2,1)}), bf16[128,768]{1,0:T(8,128)(2,1)}) %reduce-scatter.5.cloned.1.call-update) | async-done | bytes 196624 | tf_op jit(solution)/shard_map/reduce_scatter | solution.py:51
  527.3 0.0 copy-done.1
  527.3 0.0 copy-done.4
  527.3 1.2 fusion.26
  528.5 37.7 %all-reduce = (f32[128,1]{0,1:T(1,128)S(1)}, f32[128,1]{0,1:T(1,128)S(1)}) all-reduce(f32[128,1]{0,1:T(1,128)S(1)} %bitcast.24, f32[128,1]{0,1:T(1,128)S(1)} %bitcast.25), channel_id=1, replica_groups=mesh['dp'=16,'tensor'=8] {'dp'}, use_global_device_ids=true, to_apply=%region_11.0 | all-reduce | flops 256 | bytes 2048 | tf_op jit(solution)/shard_map/psum | solution.py:63
  566.1 15.2 %all-reduce.1 = (f32[768]{0:T(1024)}, f32[768]{0:T(1024)}) all-reduce(f32[768]{0:T(1024)S(1)} %get-tuple-element.8, f32[768]{0:T(1024)S(1)} %get-tuple-element.11), channel_id=1, replica_groups=mesh['dp'=16,'tensor'=8] {'tensor'}, use_global_device_ids=true, to_apply=%region_15.0 | all-reduce | flops 1536 | bytes 12288 | tf_op jit(solution)/shard_map/psum | solution.py:59
  581.4 1.8 fusion.23
  583.1 0.0 reduce-scatter.3.cloned.1.call-done
  583.1 0.0 copy-done.6
  583.1 1.6 add_convert_fusion
  (4 shorter events, 0.0 us)
Async XLA Ops:
  7.2 116.0 %all-gather.3.cloned.1.call-start = ((), (), s32[]{:S(2)}) async-start(), calls=%async_computation.2 | async-start | bytes 1769472 | tf_op jit(solution)/shard_map/all_gather | solution.py:21
  83.9 84.5 %all-gather.5.cloned.1.call-start = ((), (), s32[]{:S(2)}) async-start(), calls=%async_computation.4 | async-start | bytes 1769472 | tf_op jit(solution)/shard_map/all_gather | solution.py:23
  84.6 377.6 %all-reduce.5.cloned.1.call-start = ((), (), s32[]{:S(2)}) async-start(), calls=%async_computation.6 | async-start | bytes 25165824 | tf_op jit(solution)/shard_map/psum | solution.py:24
  177.5 284.8 %copy-start.5 = (f32[3072]{0:T(1024)S(1)}, f32[3072]{0:T(1024)}, u32[]{:S(2)}) copy-start(f32[3072]{0:T(1024)} %param.12) | copy-start | bytes 36868
  177.6 349.7 %reduce-scatter.5.cloned.1.call-start = ((), (), s32[]{:S(2)}) async-start(), calls=%async_computation.5 | async-start | bytes 1769472 | tf_op jit(solution)/shard_map/reduce_scatter | solution.py:51
  475.1 2.7 copy-start
  477.7 8.9 %copy-start.2 = (bf16[1024,768]{1,0:T(8,128)(2,1)S(1)}, bf16[1024,768]{1,0:T(8,128)(2,1)}, u32[]{:S(2)}) copy-start(bf16[1024,768]{1,0:T(8,128)(2,1)} %all-gather.5.cloned.1.call-done) | copy-start | bytes 4718596
  486.4 96.7 %reduce-scatter.3.cloned.1.call-start = ((), (), s32[]{:S(2)}) async-start(), calls=%async_computation.3 | async-start | bytes 1769472 | tf_op jit(solution)/shard_map/reduce_scatter | solution.py:28
  500.0 9.3 %slice-start = ((s8[6291456]{0:T(1024)(128)(4,1)}), s8[2097152]{0:T(1024)(128)(4,1)S(1)}, s32[]{:S(2)}) async-start(s8[6291456]{0:T(1024)(128)(4,1)} %bitcast.22), calls=%async_computation.7 | async-start | bytes 4194304
  500.0 9.3 %slice-start.1 = ((s8[6291456]{0:T(1024)(128)(4,1)}), s8[4194304]{0:T(1024)(128)(4,1)S(1)}, s32[]{:S(2)}) async-start(s8[6291456]{0:T(1024)(128)(4,1)} %bitcast.22), calls=%async_computation.8 | async-start | bytes 8388608
  500.0 9.3 %copy-start.3 = (bf16[1024,768]{1,0:T(8,128)(2,1)S(1)}, bf16[1024,768]{1,0:T(8,128)(2,1)}, u32[]{:S(2)}) copy-start(bf16[1024,768]{1,0:T(8,128)(2,1)} %all-gather.5.cloned.1.call-done) | copy-start | bytes 4718596
  509.3 18.0 %copy-start.1 = (bf16[128,768]{1,0:T(8,128)(2,1)S(1)}, bf16[128,768]{1,0:T(8,128)(2,1)}, u32[]{:S(2)}) copy-start(bf16[128,768]{1,0:T(8,128)(2,1)} %param.8) | copy-start | bytes 589828
  509.3 18.0 %copy-start.4 = (f32[768]{0:T(1024)S(1)}, f32[768]{0:T(1024)}, u32[]{:S(2)}) copy-start(f32[768]{0:T(1024)} %param.9) | copy-start | bytes 9220
  509.3 73.8 %copy-start.6 = (f32[768]{0:T(1024)S(1)}, f32[768]{0:T(1024)}, u32[]{:S(2)}) copy-start(f32[768]{0:T(1024)} %param.14) | copy-start | bytes 9220
Sparse Core Ops, SparseCore 0:
  84.0 39.0 all-gather.2
  124.8 43.5 all-gather.4
  177.7 284.5 all-reduce.4
  486.5 40.6 reduce-scatter.4
  529.5 43.9 reduce-scatter.2
where the time goes:
time: 594 us; the launch traced here: 591 us
  waiting for transfers between devices  368 us (62%)
  blocking collectives  126 us (21%)
  matrix products  58.4 us (10%)
  other arithmetic  22.2 us (4%)
  between operations  13.9 us (2%)
    psum x1, waiting for transfers between devices, on_device(): lax.psum(partial_up.astype(jnp.bfloat16), 'dp').astype(jnp.float32) + b_up  285 us
    all_gather x1, waiting for transfers between devices, on_device(): gathered = lax.all_gather(normed, 'tensor', axis=0, tiled=True)  38.4 us
    psum x1, blocking collectives, on_device(): lax.psum(jnp.sum(centred * centred, axis=1, keepdims=True), 'dp') / D  37.8 us
    psum x1, blocking collectives, on_device(): lax.psum((jnp.sum(scaled, axis=1, keepdims=True), jnp.sum(scaled * standa...  37.7 us
    all_gather x1, waiting for transfers between devices, on_device(): grad_rows = lax.all_gather(d_branch, 'tensor', axis=0, tiled=True)  36.2 us
    psum x1, blocking collectives, on_device(): centre = lax.psum(jnp.sum(widened, axis=1, keepdims=True), 'dp') / D  34.8 us
    psum x1, blocking collectives, on_device(): lax.psum((jnp.sum(grad_normed * standard, axis=0), jnp.sum(grad_normed, a...  15.2 us
    reduce_sum x1, other arithmetic, on_device(): grad_b_up = jnp.sum(grad_hidden.astype(jnp.float32), axis=0)  12.8 us
  transfers between devices with their start and end apart: 5, of which 4 were waited for; matrix products, arithmetic and copies ran while one was open for 8% of the time, Pallas kernels for 0%

commit v1 on v0

v1 whole, which is shorter than its diff:
```python
import functools

import jax
import jax.numpy as jnp
from jax import lax
from jax.experimental import pallas as pl
from jax.experimental.pallas import tpu as pltpu
from jax.sharding import PartitionSpec as P

MESH = pl.DeviceIdType.MESH
F32, BF16 = jnp.float32, jnp.bfloat16

D = 12288
N_X, N_Y = 4, 4
WIDE = 768
HALF = 1536
CHUNKS = 4
ROWS = 256
OWN = 32
TILE = 512
K0 = 0.7978845608028654
K1 = 0.044715


def transposed_dot(left, right):
    return lax.dot_general(left, right, (((1,), (1,)), ((), ())), preferred_element_type=F32)


def columns_to_rows(first, second):
    lane = lax.broadcasted_iota(jnp.int32, (128, 128), 1)
    return jnp.where(lane == 0, first, jnp.where(lane == 1, second, 0.0)).T[0:8, :]


def rows_to_columns(first, second):
    row = lax.broadcasted_iota(jnp.int32, (128, 128), 0)
    both = jnp.where(row == 0, first, jnp.where(row == 1, second, 0.0)).T
    return both[:, 0:1], both[:, 1:2]


def kernel(
    x_ref, gain_ref, bias_ref, b_up_ref, b_down_ref, d_ref, w_up_hbm, w_down_hbm,
    branch_ref, grad_in_ref, grad_gain_ref, grad_bias_ref, act_hbm, gh_hbm, nrm_hbm, dbr_hbm,
    w_up, w_down, dbr, nrm, part, core_in, x1_in, x2_in, z_in, full, t_out, t_in,
    standard, grad_normed, stats, back_stats, gb,
    load_sem, store_sem, t_send, t_recv, core_send, core_recv, x1_send, x1_recv, x2_send, x2_recv,
    z_send, z_recv, gz_send, gz_recv, gx_send, gx_recv, gf_send, gf_recv, gc_send, gc_recv,
    ts_send, ts_recv, st_send, st_recv, bs_send, bs_recv, gb_send, gb_recv,
):
    dp, tensor = lax.axis_index("dp"), lax.axis_index("tensor")
    xi, zh, core = dp // 4, (dp // 2) % 2, dp % 2
    yi, zl = tensor // 2, tensor % 2
    right = (((xi + 1) % 4) * 4 + zh * 2 + core, tensor)
    left = (((xi + 3) % 4) * 4 + zh * 2 + core, tensor)
    across = (xi * 4 + (1 - zh) * 2 + core, tensor)
    sibling = (xi * 4 + zh * 2 + (1 - core), tensor)
    x_right, x_left, x_far = (xi + 1) % 4, (xi + 3) % 4, (xi + 2) % 4

    t_to = []
    for dy in range(4):
        for dz in range(2):
            if dy or dz:
                t_to.append((dp, ((yi + dy) % 4) * 2 + (1 - zl if dz else zl)))
    d_to = []
    for dx in range(4):
        for mz in range(2):
            for mc in range(2):
                if dx or mz or mc:
                    d_to.append((((xi + dx) % 4) * 4 + (1 - zh if mz else zh) * 2 + (1 - core if mc else core), tensor))

    load_down = pltpu.make_async_copy(w_down_hbm, w_down, load_sem.at[0])
    load_down.start()
    load_up = [pltpu.make_async_copy(w_up_hbm.at[:, pl.ds(h * HALF, HALF)], w_up.at[h], load_sem.at[1 + h]) for h in range(2)]
    for copy in load_up:
        copy.start()

    barrier = pltpu.get_barrier_semaphore()
    for device in t_to + d_to:
        pl.semaphore_signal(barrier, inc=1, device_id=device, device_id_type=MESH)

    for c in range(CHUNKS):
        dbr[c, pl.ds(tensor * OWN, OWN), :] = d_ref[c * OWN : (c + 1) * OWN, :]
    pl.semaphore_wait(barrier, len(t_to) + len(d_to))

    sent = []

    def send(source, target, send_sem, recv_sem, device):
        copy = pltpu.make_async_remote_copy(
            src_ref=source, dst_ref=target, send_sem=send_sem, recv_sem=recv_sem, device_id=device, device_id_type=MESH
        )
        copy.start()
        sent.append(copy)
        return copy

    def gather_tokens(array, which):
        made = []
        for c in range(CHUNKS):
            place = array.at[c, pl.ds(tensor * OWN, OWN)]
            made.append([send(place, place, t_send.at[which, c, s], t_recv.at[which, c, s], device) for s, device in enumerate(t_to)])
        return made

    dbr_copies = gather_tokens(dbr, 0)

    widened = x_ref[...].astype(F32)
    total = jnp.sum(widened, axis=1, keepdims=True)
    off = widened - total / WIDE
    stats[0] = columns_to_rows(total, jnp.sum(off * off, axis=1, keepdims=True))
    stat_copies = [send(stats.at[0], stats.at[s + 1], st_send.at[s], st_recv.at[s], device) for s, device in enumerate(d_to)]

    def normalise():
        for copy in stat_copies:
            copy.wait_recv()
        sums = [stats[s, 0:1, :] for s in range(16)]
        mean = functools.reduce(jnp.add, sums) / D
        spread = jnp.zeros_like(mean)
        for s in range(16):
            apart = sums[s] / WIDE - mean
            spread = spread + (stats[s, 1:2, :] + WIDE * (apart * apart))
        inverse_row = lax.rsqrt(spread / D + 1e-05)
        mean, inverse = rows_to_columns(mean, inverse_row)
        for c in range(CHUNKS):
            rows = slice(c * OWN, (c + 1) * OWN)
            std = (x_ref[rows, :].astype(F32) - mean[rows]) * inverse[rows]
            standard[rows, :] = std
            nrm[c, pl.ds(tensor * OWN, OWN), :] = (std * gain_ref[...] + bias_ref[...]).astype(BF16)
        return inverse, gather_tokens(nrm, 1)

    core_copies, x1_copies, x2_copies, z_copies = {}, {}, {}, {}

    def multiply(u):
        c, k = u // 2, u % 2
        source = nrm if k else dbr
        for s in (nrm_copies if k else dbr_copies)[c]:
            s.wait_recv()
        for step in range(2):
            half = (1 - core) if step == 0 else core

            def tile(j, _):
                at = pl.multiple_of(j * TILE, TILE)
                if k:
                    value = jnp.dot(source[c], w_up[half, :, pl.ds(at, TILE)], preferred_element_type=F32)
                else:
                    value = transposed_dot(source[c], w_down[half, pl.ds(at, TILE), :])
                part[u, half, :, pl.ds(at, TILE)] = value.astype(BF16)
                return 0

            lax.fori_loop(0, HALF // TILE, tile, 0)
            if step == 0:
                core_copies[u] = send(part.at[u, half], core_in.at[u], core_send.at[u], core_recv.at[u], sibling)

    def add_core(u):
        core_copies[u].wait_recv()

        def block(i, _):
            rows = pl.ds(pl.multiple_of(i * 16, 16), 16)
            part[u, core, rows, :] = (part[u, core, rows, :].astype(F32) + core_in[u, rows, :].astype(F32)).astype(BF16)
            return 0

        lax.fori_loop(0, ROWS // 16, block, 0)
        x1_copies[u] = [
            send(part.at[u, core, pl.ds(x_far * 64, 32)], x1_in.at[u, 0], x1_send.at[u, 0], x1_recv.at[u, 0], right),
            send(part.at[u, core, pl.ds(x_far * 64 + 32, 32)], x1_in.at[u, 1], x1_send.at[u, 1], x1_recv.at[u, 1], left),
        ]

    def add_x1(u):
        x2_copies[u] = []
        for side, (piece, device) in enumerate(((x_right, right), (x_left, left))):
            x1_copies[u][side].wait_recv()
            for i in range(2):
                rows = pl.ds(pl.multiple_of(piece * 64 + side * 32 + i * 16, 16), 16)
                there = x1_in[u, side, i * 16 : (i + 1) * 16, :]
                part[u, core, rows, :] = (part[u, core, rows, :].astype(F32) + there.astype(F32)).astype(BF16)
            x2_copies[u].append(
                send(part.at[u, core, pl.ds(piece * 64, 64)], x2_in.at[u, side], x2_send.at[u, side], x2_recv.at[u, side], device)
            )

    def add_x2(u):
        for copy in x2_copies[u]:
            copy.wait_recv()
        for sub in (1 - zh, zh):
            for i in range(2):
                at = pl.multiple_of(sub * 32 + i * 16, 16)
                rows = pl.ds(pl.multiple_of(xi * 64 + at, 16), 16)
                there = x2_in[u, 0, pl.ds(at, 16), :].astype(F32) + x2_in[u, 1, pl.ds(at, 16), :].astype(F32)
                part[u, core, rows, :] = (part[u, core, rows, :].astype(F32) + there).astype(BF16)
            if sub is not zh:
                place = part.at[u, core, pl.ds(xi * 64 + (1 - zh) * 32, 32)]
                z_copies[u] = send(place, z_in.at[u], z_send.at[u], z_recv.at[u], across)

    gz, gx, gf, gc = {}, {}, {}, {}
    mine = xi * 64 + zh * 32

    def activate(c):
        z_copies[2 * c].wait_recv()
        z_copies[2 * c + 1].wait_recv()
        bias = b_up_ref[core]
        for i in range(2):
            rows = pl.ds(pl.multiple_of(mine + i * 16, 16), 16)
            here = slice(i * 16, (i + 1) * 16)
            ga = part[2 * c, core, rows, :].astype(F32) + z_in[2 * c, here, :].astype(F32)
            h = part[2 * c + 1, core, rows, :].astype(F32) + z_in[2 * c + 1, here, :].astype(F32) + bias
            square = h * h
            t = jnp.tanh(K0 * (h + K1 * (square * h)))
            full[0, c, core, rows, :] = (0.5 * h * (1.0 + t)).astype(BF16)
            slope = 0.5 * (1.0 + t) + 0.5 * h * (1.0 - t * t) * (K0 * (1.0 + 3.0 * K1 * square))
            full[1, c, core, rows, :] = (ga * slope).astype(BF16)
        for k in range(2):
            place = full.at[k, c, core, pl.ds(mine, 32)]
            gz[k, c] = send(place, place, gz_send.at[k, c], gz_recv.at[k, c], across)

    def to_sibling(k, c, slot, piece):
        place = full.at[k, c, core, pl.ds(piece * 64, 64)]
        gc[k, c, slot] = send(place, place, gc_send.at[k, c, slot], gc_recv.at[k, c, slot], sibling)

    def gather_x(c):
        for k in range(2):
            gz[k, c].wait_recv()
            place = full.at[k, c, core, pl.ds(xi * 64, 64)]
            for side, device in enumerate((right, left)):
                gx[k, c, side] = send(place, place, gx_send.at[k, c, side], gx_recv.at[k, c, side], device)
            to_sibling(k, c, 0, xi)

    def forward_x(c):
        for k in range(2):
            for side, (piece, device) in enumerate(((x_left, right), (x_right, left))):
                gx[k, c, side].wait_recv()
                place = full.at[k, c, core, pl.ds(piece * 64 + side * 32, 32)]
                gf[k, c, side] = send(place, place, gf_send.at[k, c, side], gf_recv.at[k, c, side], device)
                to_sibling(k, c, 1 + side, piece)

    def last_x(c):
        for k in range(2):
            for side in range(2):
                gf[k, c, side].wait_recv()
            to_sibling(k, c, 3, x_far)

    stores, ts = [], {}

    def store(source, target, index):
        copy = pltpu.make_async_copy(source, target, store_sem.at[index])
        copy.start()
        stores.append(copy)

    def multiply_back(c):
        for k in range(2):
            for slot in range(4):
                gc[k, c, slot].wait_recv()

            def tile(j, _):
                at = pl.multiple_of(j * 256, 256)
                if k:
                    value = transposed_dot(full[1, c, 0], w_up[0, pl.ds(at, 256), :])
                    value += transposed_dot(full[1, c, 1], w_up[1, pl.ds(at, 256), :])
                else:
                    value = jnp.dot(full[0, c, 0], w_down[0, :, pl.ds(at, 256)], preferred_element_type=F32)
                    value += jnp.dot(full[0, c, 1], w_down[1, :, pl.ds(at, 256)], preferred_element_type=F32)
                t_out[k, c, :, pl.ds(at, 256)] = value.astype(BF16)
                return 0

            lax.fori_loop(0, WIDE // 256, tile, 0)
            for s, device in enumerate(t_to):
                place = t_out.at[k, c, pl.ds(device[1] * OWN, OWN)]
                ts[k, c, s] = send(place, t_in.at[k, c, s], ts_send.at[k, c, s], ts_recv.at[k, c, s], device)
            for half in range(2):
                target = (gh_hbm if k else act_hbm).at[pl.ds(c * ROWS, ROWS), pl.ds(half * HALF, HALF)]
                store(full.at[k, c, half], target, (k * CHUNKS + c) * 2 + half)

    def finish_tokens(c):
        for k in range(2):
            for s in range(7):
                ts[k, c, s].wait_recv()
            value = t_out[k, c, pl.ds(pl.multiple_of(tensor * OWN, OWN), OWN), :].astype(F32)
            for s in range(7):
                value = value + t_in[k, c, s].astype(F32)
            rows = slice(c * OWN, (c + 1) * OWN)
            if k:
                grad_normed[rows, :] = value
            else:
                branch_ref[rows, :] = (value + b_down_ref[...]).astype(BF16)

    units = 2 * CHUNKS
    load_down.wait()
    inverse = None
    for slot in range(-1, units + 8):
        if 0 <= slot + 1 < units:
            if slot + 1 == 1:
                inverse, nrm_copies = normalise()
                for copy in load_up:
                    copy.wait()
            multiply(slot + 1)
            add_core(slot + 1)
        if 0 <= slot < units:
            add_x1(slot)
        if 0 <= slot - 1 < units:
            add_x2(slot - 1)
        for offset, step in ((3, activate), (4, gather_x), (5, forward_x), (6, last_x), (7, multiply_back), (8, finish_tokens)):
            c, rest = divmod(slot - offset, 2)
            if 0 <= c < CHUNKS and rest == 0:
                step(c)

    for c in range(CHUNKS):
        store(dbr.at[c], dbr_hbm.at[pl.ds(c * ROWS, ROWS)], 16 + c)
        store(nrm.at[c], nrm_hbm.at[pl.ds(c * ROWS, ROWS)], 20 + c)

    gn = grad_normed[...]
    std = standard[...]
    scaled = gn * gain_ref[...]
    back_stats[0] = columns_to_rows(
        jnp.sum(scaled, axis=1, keepdims=True), jnp.sum(scaled * std, axis=1, keepdims=True)
    )
    back_copies = [
        send(back_stats.at[0], back_stats.at[s + 1], bs_send.at[s], bs_recv.at[s], device) for s, device in enumerate(d_to)
    ]
    gb[0, 0:1, :] = jnp.sum(gn * std, axis=0, keepdims=True)
    gb[0, 1:2, :] = jnp.sum(gn, axis=0, keepdims=True)
    gb[0, 2:8, :] = jnp.zeros((6, WIDE), F32)
    gb_copies = [send(gb.at[0], gb.at[s + 1], gb_send.at[s], gb_recv.at[s], device) for s, device in enumerate(t_to)]
    for copy in back_copies:
        copy.wait_recv()
    first = functools.reduce(jnp.add, [back_stats[s, 0:1, :] for s in range(16)]) / D
    second = functools.reduce(jnp.add, [back_stats[s, 1:2, :] for s in range(16)]) / D
    first, second = rows_to_columns(first, second)
    grad_in_ref[...] = (inverse * (scaled - first - std * second)).astype(BF16)
    for copy in gb_copies:
        copy.wait_recv()
    both = functools.reduce(jnp.add, [gb[s] for s in range(8)])
    grad_gain_ref[...] = both[0:1, :]
    grad_bias_ref[...] = both[1:2, :]

    for copy in stores:
        copy.wait()
    for copy in sent:
        copy.wait_send()


def on_device(inputs, norm_gain, norm_bias, w_up, b_up, w_down, b_down, d_branch):
    vmem = pl.BlockSpec(memory_space=pltpu.VMEM)
    hbm = pl.BlockSpec(memory_space=pl.ANY)
    units = 2 * CHUNKS
    dma = pltpu.SemaphoreType.DMA
    shape = jax.ShapeDtypeStruct
    branch, grad_inputs, grad_gain, grad_bias, act, gh, nrm, dbr = pl.pallas_call(
        kernel,
        out_shape=(
            shape((128, WIDE), BF16), shape((128, WIDE), BF16), shape((1, WIDE), F32), shape((1, WIDE), F32),
            shape((1024, 2 * HALF), BF16), shape((1024, 2 * HALF), BF16), shape((1024, WIDE), BF16), shape((1024, WIDE), BF16),
        ),
        in_specs=[vmem] * 6 + [hbm] * 2,
        out_specs=(vmem,) * 4 + (hbm,) * 4,
        scratch_shapes=[
            pltpu.VMEM((2, WIDE, HALF), BF16),
            pltpu.VMEM((2, HALF, WIDE), BF16),
            pltpu.VMEM((CHUNKS, ROWS, WIDE), BF16),
            pltpu.VMEM((CHUNKS, ROWS, WIDE), BF16),
            pltpu.VMEM((units, 2, ROWS, HALF), BF16),
            pltpu.VMEM((units, ROWS, HALF), BF16),
            pltpu.VMEM((units, 2, 32, HALF), BF16),
            pltpu.VMEM((units, 2, 64, HALF), BF16),
            pltpu.VMEM((units, 32, HALF), BF16),
            pltpu.VMEM((2, CHUNKS, 2, ROWS, HALF), BF16),
            pltpu.VMEM((2, CHUNKS, ROWS, WIDE), BF16),
            pltpu.VMEM((2, CHUNKS, 7, OWN, WIDE), BF16),
            pltpu.VMEM((128, WIDE), F32),
            pltpu.VMEM((128, WIDE), F32),
            pltpu.VMEM((16, 8, 128), F32),
            pltpu.VMEM((16, 8, 128), F32),
            pltpu.VMEM((8, 8, WIDE), F32),
            dma((3,)), dma((24,)),
            dma((2, CHUNKS, 7)), dma((2, CHUNKS, 7)),
            dma((units,)), dma((units,)),
            dma((units, 2)), dma((units, 2)),
            dma((units, 2)), dma((units, 2)),
            dma((units,)), dma((units,)),
            dma((2, CHUNKS)), dma((2, CHUNKS)),
            dma((2, CHUNKS, 2)), dma((2, CHUNKS, 2)),
            dma((2, CHUNKS, 2)), dma((2, CHUNKS, 2)),
            dma((2, CHUNKS, 4)), dma((2, CHUNKS, 4)),
            dma((2, CHUNKS, 7)), dma((2, CHUNKS, 7)),
            dma((15,)), dma((15,)), dma((15,)), dma((15,)), dma((7,)), dma((7,)),
        ],
        compiler_params=pltpu.CompilerParams(collective_id=0, has_side_effects=True, vmem_limit_bytes=62 * 2**20),
    )(
        inputs, norm_gain.reshape(1, WIDE), norm_bias.reshape(1, WIDE), b_up.reshape(2, 1, HALF), b_down.reshape(1, WIDE), d_branch,
        w_up, w_down.reshape(2, HALF, WIDE),
    )
    grad_w_down = lax.dot_general(act, dbr, (((0,), (0,)), ((), ())), preferred_element_type=F32).astype(BF16)
    grad_w_up = lax.dot_general(nrm, gh, (((0,), (0,)), ((), ())), preferred_element_type=F32).astype(BF16)
    grad_b_down = jnp.sum(dbr.astype(F32), axis=0)
    grad_b_up = jnp.sum(gh.astype(F32), axis=0)
    return branch, grad_inputs, grad_w_up, grad_b_up, grad_w_down, grad_b_down, grad_gain.reshape(WIDE), grad_bias.reshape(WIDE)


def solution(mesh):
    placed = (
        P("tensor", "dp"), P("dp"), P("dp"), P("dp", "tensor"), P("tensor"), P("tensor", "dp"), P("dp"), P("tensor", "dp"),
    )
    return jax.shard_map(
        on_device,
        mesh=mesh,
        in_specs=placed,
        out_specs=(
            P("tensor", "dp"), P("tensor", "dp"), P("dp", "tensor"), P("tensor"), P("tensor", "dp"), P("dp"), P("dp"), P("dp"),
        ),
        check_vma=False,
    )
```

time: 594 us -> 203 us (0.34)
  waiting for transfers between devices: 368 us -> 0 us
  Pallas kernels: 0 us -> 177 us
  blocking collectives: 126 us -> 0 us
  matrix products: 58.4 us -> 16.2 us
  other arithmetic: 22.2 us -> 3.62 us
  between operations: 13.9 us -> 0.68 us
    psum x1 -> x0, waiting for transfers between devices: 285 us -> none  [on_device(): lax.psum(partial_up.astype(jnp.bfloat16), 'dp').astype(jnp.float32) + b_up]
    pallas_call x0 -> x1, Pallas kernels: none -> 177 us  [on_device(): pl.pallas_call(kernel, out_shape=(shape((128, WIDE), BF16), shape((128, W...]
    psum x4 -> x0, blocking collectives: 126 us -> none  [the longest x1 37.8 us: on_device(): lax.psum(jnp.sum(centred * centred, axis=1, keepdims=True), 'dp') / D]
    all_gather x2 -> x0, waiting for transfers between devices: 74.7 us -> none  [the longest x1 38.4 us: on_device(): gathered = lax.all_gather(normed, 'tensor', axis=0, tiled=True)]
    dot_general x6 -> x2, matrix products: 58.4 us -> 16.2 us  [the longest x1 9.46 us: on_device(): lax.dot_general(act, dbr, (((0,), (0,)), ((), ())), preferred_element_typ...]
    reduce_sum x5 -> x2, other arithmetic: 17 us -> 2.41 us  [the longest x1 1.53 us: on_device(): grad_b_up = jnp.sum(gh.astype(F32), axis=0)]
    reduce_scatter x2 -> x0, waiting for transfers between devices: 8.06 us -> none  [the longest x1 8.06 us: on_device(): lax.psum_scatter(lax.dot_general(rows_part, w_up, (((1,), (1,)), ((), ())...]
  transfers between devices with their start and end apart: 5 -> 0, of which waited for: 4 -> 0; matrix products, arithmetic and copies ran while one was open for 8% -> 0% of each run, Pallas kernels for 0% -> 0%
where the time goes in v1:
time: 203 us
  Pallas kernels  177 us (87%)
  matrix products  16.2 us (8%)
  local copies, waits for them, and re-layouts  5.18 us (3%)
  other arithmetic  3.62 us (2%)
    pallas_call x1, Pallas kernels, on_device(): pl.pallas_call(kernel, out_shape=(shape((128, WIDE), BF16), shape((128, W...  177 us
    dot_general x1, matrix products, on_device(): lax.dot_general(act, dbr, (((0,), (0,)), ((), ())), preferred_element_typ...  9.46 us
    dot_general x1, matrix products, on_device(): lax.dot_general(nrm, gh, (((0,), (0,)), ((), ())), preferred_element_type...  6.79 us

profile of v1, /device:TPU:1, one launch (start us, length us, event | category | flops | bytes accessed | tf_op | source)
XLA Modules:
  0.0 203.2 jit_solution(14303123447035272637)
XLA Ops:
  0.6 1.3 reshape.37.gain_ref
  1.9 1.3 reshape.38.bias_ref
  3.2 1.3 reshape.40.b_down_ref
  4.4 177.5 %shard_map.143 = (bf16[128,768]{1,0:T(8,128)(2,1)}, bf16[128,768]{1,0:T(8,128)(2,1)}, f32[1,768]{1,0:T(1,128)}, f32[1,768]{1,0:T(1,128)}, bf16[1024,3072]{1,0:T(...) custom-call(bf16[128,768]{1,0:T(8,128)(2,1)} %x_ref.1, ...), custom_call_target="tpu_custom_call" | custom-call | tf_op jit(solution)/shard_map/pallas_call | solution.py:341
  181.9 0.0 copy-start
  181.9 0.0 copy-start.6
  181.9 9.5 %convolution_convert_fusion = bf16[3072,768]{1,0:T(8,128)(2,1)} fusion(bf16[1024,3072]{1,0:T(8,128)(2,1)} %get-tuple-element.20, bf16[1024,768]{1,0:T(8,128)(2,1)} %get-tuple-element.21), kind=kOutput, calls=%fused_computation.1 | convolution fusion | flops 4834197504 | bytes 12582912 | tf_op jit(solution)/shard_map/dot_general | solution.py:385
  191.4 0.0 copy-done
  191.4 0.0 copy-done.6
  191.4 6.8 %convolution_convert_fusion.1 = bf16[768,3072]{1,0:T(8,128)(2,1)} fusion(bf16[1024,768]{1,0:T(8,128)(2,1)S(1)} %copy-done.6, bf16[1024,3072]{1,0:T(8,128)(2,1)S(1)} %copy-done), kind=kOutput, calls=%fused_computation.2 | convolution fusion | flops 4834197504 | bytes 12582912 | tf_op jit(solution)/shard_map/dot_general | solution.py:386
  198.2 0.0 copy-start.1
  198.2 0.0 copy-start.5
  198.2 0.0 copy-start.4
  198.2 0.0 copy-start.3
  198.2 0.0 copy-start.2
  198.2 1.5 convert_reduce_fusion
  199.8 0.0 copy-done.1
  199.8 0.9 convert_reduce_fusion.1
  200.6 0.0 copy-done.5
  200.6 0.6 reduce
  201.2 0.0 copy-done.4
  201.2 0.6 reduce.1
  201.9 0.0 copy-done.3
  201.9 0.7 copy.18
  202.5 0.0 copy-done.2
  202.5 0.7 copy.19
Async XLA Ops:
  181.9 9.5 %copy-start = (bf16[1024,3072]{1,0:T(8,128)(2,1)S(1)}, bf16[1024,3072]{1,0:T(8,128)(2,1)}, u32[]{:S(2)}) copy-start(bf16[1024,3072]{1,0:T(8,128)(2,1)} %get-tuple-element.19) | copy-start | bytes 18874372
  181.9 9.5 %copy-start.6 = (bf16[1024,768]{1,0:T(8,128)(2,1)S(1)}, bf16[1024,768]{1,0:T(8,128)(2,1)}, u32[]{:S(2)}) copy-start(bf16[1024,768]{1,0:T(8,128)(2,1)} %get-tuple-element.18) | copy-start | bytes 4718596
  198.2 1.6 copy-start.1
  198.2 2.4 %copy-start.5 = (f32[1,768]{1,0:T(1,128)S(1)}, f32[1,768]{1,0:T(1,128)}, u32[]{:S(2)}) copy-start(f32[1,768]{1,0:T(1,128)} %get-tuple-element.22) | copy-start | bytes 9220
  198.2 3.0 %copy-start.4 = (f32[1,768]{1,0:T(1,128)S(1)}, f32[1,768]{1,0:T(1,128)}, u32[]{:S(2)}) copy-start(f32[1,768]{1,0:T(1,128)} %get-tuple-element.23) | copy-start | bytes 9220
  198.2 3.6 %copy-start.3 = (bf16[128,768]{1,0:T(8,128)(2,1)S(1)}, bf16[128,768]{1,0:T(8,128)(2,1)}, u32[]{:S(2)}) copy-start(bf16[128,768]{1,0:T(8,128)(2,1)} %get-tuple-element.32) | copy-start | bytes 589828
  198.2 4.3 %copy-start.2 = (bf16[128,768]{1,0:T(8,128)(2,1)S(1)}, bf16[128,768]{1,0:T(8,128)(2,1)}, u32[]{:S(2)}) copy-start(bf16[128,768]{1,0:T(8,128)(2,1)} %get-tuple-element.33) | copy-start | bytes 589828
